TPU v7x, 128 devices: a whole 4x4x4 slice. The times are simulated.
128 devices in a mesh: blk: 8 (over x, core), inner: 16 (over y, z).
Axes of the slice: x: 4, y: 4, z: 4, core: 2. Of those that a mesh axis runs over, the one named last changes fastest.
Arguments:
- sheet_plasma_quantities: float32 [8, 4, 1024, 2048], P(None, None, 'blk', 'inner'), may hold values from -6 to 6
- speeds: float32 [3, 4, 1024, 2048], P(None, None, 'blk', 'inner'), may hold values from -1 to 1
- source_matrix: float32 [8, 8], replicated, may hold values from -2 to 2
- pedersen: float32 [2048, 4096], P('blk', 'inner'), may hold values from 0.05 to 1
- owners: int32 [32768, 1], P(('blk', 'inner')), may hold values from 0 to 127; in each aligned block of 256 rows (0 to 255, 256 to 511, ...) at most 4 rows name the same one
- tile_positions: int32 [32768], P(('blk', 'inner')), may hold values from 0 to 1023
Outputs:
- updated_plasma_quantities: float32 [8, 4, 1024, 2048], P(None, None, 'blk', 'inner')
- potential: float32 [2048, 4096], P('blk', 'inner')
- heating: float32 [2048, 4096], P('blk', 'inner')
- block_potential_heat: float32 [32768, 128], P(('blk', 'inner'))
Inputs may be any that keep to these rules, and one draw needn't show every extreme that they name: `owners`: within the rows of one device (aligned blocks of 256 boundary blocks) no owner is named more than 4 times.
All inputs are finite; a program needn't handle non-finite values.
Results may differ from a plain program's by a relative error of at most 0.00045.
Values sent between devices are 32-bit elements; how exact they have to be, the bound alone decides.
A program may use at most 192 MiB of HBM per device.

v0:
```python
import functools
import math

import jax
import jax.numpy as jnp
import numpy as np
from jax import lax
from jax.experimental import pallas as pl
from jax.experimental.pallas import tpu as pltpu
from jax.sharding import PartitionSpec as P

F32 = jnp.float32
BF16 = jnp.bfloat16
I32 = jnp.int32
MESH = pl.DeviceIdType.MESH
BLOCK = 8
PAIRS = 8
SCREENING = 2.0
GAIN = 4096.0
VMEM_LIMIT = 60 * 1024 * 1024


def iota(shape, dim):
    return lax.broadcasted_iota(I32, shape, dim)


def split(value):
    high = value.astype(BF16)
    return high, (value - high.astype(F32)).astype(BF16)


def split3(value):
    high = value.astype(BF16)
    rest = value - high.astype(F32)
    middle = rest.astype(BF16)
    return high, middle, (rest - middle.astype(F32)).astype(BF16)


def dot(left, right, dims=((1,), (0,))):
    return lax.dot_general(left, right, (dims, ((), ())), preferred_element_type=F32)


def dot3(left, right, dims):
    lh, ll = left
    rh, rl = right
    return dot(lh, rh, dims) + dot(ll, rh, dims) + dot(lh, rl, dims)


def spectral_tables(blk_count, inner_count, lat_dev, lon_dev):
    orders = PAIRS * 2 * inner_count
    degrees = orders
    lon_total = lon_dev * inner_count
    first = np.arange(inner_count * PAIRS).reshape(inner_count, 1, PAIRS)
    order_of = np.concatenate([first, orders - 1 - first], axis=1).reshape(-1)
    cols = np.arange(lon_dev)
    phase = (order_of[:, None] * cols[None, :] % lon_total) * (2.0 * math.pi / lon_total)
    wave = np.stack([np.cos(phase), np.sin(phase)]).astype(np.float32)
    turn = (order_of[:, None] * (np.arange(inner_count) * lon_dev)[None, :] % lon_total) * (
        2.0 * math.pi / lon_total
    )
    twiddle = np.zeros((order_of.shape[0], 128), np.float32)
    twiddle[:, :inner_count] = np.cos(turn)
    twiddle[:, 32 : 32 + inner_count] = np.sin(turn)
    twiddle[:, 64] = order_of
    twiddle[:, 65] = np.where(order_of == 0, 1.0, 2.0)

    turns = -(-(degrees + 1) // 16)
    steps = turns * 16
    table = np.zeros((inner_count, turns + 1, PAIRS, 128), np.float32)

    def up(degree, order):
        return np.sqrt(
            np.float32(4.0 * degree * degree - 1.0) / np.float32(degree * degree - order * order)
        )

    counter = np.arange(1, orders, dtype=np.float64)
    log_start = 0.5 * np.log(0.5) + np.concatenate(
        [np.zeros(1), np.cumsum(0.5 * np.log((2.0 * counter + 1.0) / (2.0 * counter)))]
    )
    for pair in range(inner_count * PAIRS):
        place, lane = divmod(pair, PAIRS)
        low, partner = pair, orders - 1 - pair
        table[place, turns, lane, :4] = [low, log_start[low], partner, log_start[partner]]
        for step in range(degrees + 1):
            if step <= low:
                order, degree, kind = partner, partner + step, 3
            else:
                order, degree, kind = low, step - 1, 2
            turn_at, offset = divmod(step, 16)
            if degree == order:
                table[place, turn_at, lane, kind * 16 + offset] = 1.0
                continue
            ratio = up(degree, order)
            table[place, turn_at, lane, offset] = ratio
            if degree >= order + 2:
                table[place, turn_at, lane, 16 + offset] = ratio / up(degree - 1, order)
    return wave, twiddle, table, steps


def kernel(
    sizes,
    u_hbm,
    w_hbm,
    mix_ref,
    ped_hbm,
    owner_ref,
    tile_ref,
    wave_hbm,
    twiddle_hbm,
    table_hbm,
    out_ref,
    pot_ref,
    heat_ref,
    blocks_ref,
    u_ref,
    w_ref,
    ped_ref,
    wave_ref,
    twiddle_ref,
    ratios,
    coef,
    u1,
    first_send_x,
    first_send_y,
    first_recv_x,
    first_recv_y,
    rest_send_x,
    rest_send_y,
    rest_recv_x,
    rest_recv_y,
    face_send_x,
    face_send_y,
    face_recv_x,
    face_recv_y,
    ring_x,
    corner_send,
    corner_recv,
    last_send_x,
    last_send_y,
    last_recv_x,
    last_recv_y,
    turned,
    sel_t,
    label_ref,
    face_send,
    face_recv,
    forcing,
    base_ref,
    values_ref,
    spec_send,
    spec_recv,
    leg,
    mask_ref,
    coef_send,
    coef_recv,
    syn_all,
    rim_send,
    rim_recv,
    grids,
    wide,
    reply_send,
    reply_recv,
    edge_sems,
    send_sems,
    recv_sems,
    rim_sems,
    corner_sems,
    in_sems,
    ready,
):
    na, nb, steps = sizes
    count = na * nb
    lat, lon = ped_ref.shape
    rows_total, cols_total = lat * na, lon * nb
    cap = face_send.shape[1]
    slots = count * cap
    a, b = lax.axis_index("blk"), lax.axis_index("inner")
    me = a * nb + b
    orders = PAIRS * 2 * nb
    spec_rows = 2 * orders

    nx, nz = na // 2, min(4, nb)
    ny = nb // nz
    chip_x, core, chip_y, chip_z = a // 2, lax.rem(a, 2), b // nz, lax.rem(b, nz)
    peer_a = {
        (dx, dc): lax.rem(chip_x + dx, nx) * 2 + lax.rem(core + dc, 2)
        for dx in range(nx)
        for dc in range(2)
    }
    peer_b = {
        (dy, dz): lax.rem(chip_y + dy, ny) * nz + lax.rem(chip_z + dz, nz)
        for dy in range(ny)
        for dz in range(nz)
    }

    def hops(move):
        dx, dc, dy, dz = move
        return 2 * (min(dx, nx - dx) + min(dy, ny - dy) + min(dz, nz - dz)) + dc

    moves = sorted(
        [(dx, dc, dy, dz) for dx, dc in peer_a for dy, dz in peer_b if (dx, dc, dy, dz) != (0, 0, 0, 0)],
        key=hops,
        reverse=True,
    )
    blk_moves = [move for move in moves if move[2:] == (0, 0)]
    inner_moves = [move for move in moves if move[:2] == (0, 0)]

    def device(move):
        return peer_a[move[:2]], peer_b[move[2:]]

    def remote(src, dst, send_sem, recv_sem, target):
        pltpu.make_async_remote_copy(
            src_ref=src,
            dst_ref=dst,
            send_sem=send_sem,
            recv_sem=recv_sem,
            device_id=target,
            device_id_type=MESH,
        ).start()

    def take(ref, sem):
        pltpu.make_async_copy(ref, ref, sem).wait()

    def signal(sem, target):
        pl.semaphore_signal(sem, inc=1, device_id=target, device_id_type=MESH)

    up_a, down_a = lax.rem(a + 1, na), lax.rem(a + na - 1, na)
    up_b, down_b = lax.rem(b + 1, nb), lax.rem(b + nb - 1, nb)

    barrier = pltpu.get_barrier_semaphore()
    y_moves = [move for move in inner_moves if move[3] == 0]
    z_moves = [move for move in inner_moves if move[2] == 0]
    greeted = [device(move) for move in blk_moves + y_moves + z_moves]
    greeted += [(a, up_b), (a, down_b)]
    corners = [(up_a, up_b), (up_a, down_b), (down_a, up_b), (down_a, down_b)]
    greeted += corners
    for target in greeted:
        signal(barrier, target)
    fetches = [
        pltpu.make_async_copy(src, dst, in_sems.at[at])
        for at, (src, dst) in enumerate(
            [
                (w_hbm, w_ref),
                (u_hbm.at[:, pl.ds(0, 2)], u_ref.at[:, pl.ds(0, 2)]),
                (twiddle_hbm, twiddle_ref),
                (wave_hbm, wave_ref),
                (table_hbm.at[b], ratios),
                (ped_hbm, ped_ref),
                (u_hbm.at[:, pl.ds(2, 2)], u_ref.at[:, pl.ds(2, 2)]),
            ]
        )
    ]
    for at in (0, 1, 6, 2, 3, 4, 5):
        fetches[at].start()

    row = iota((128, 128), 0)
    lane = iota((128, 128), 1)
    row8 = iota((8, 128), 0)
    fetches[0].wait()

    def make_coef(z, carry):
        wx, wy = 0.15 * w_ref[0, z], 0.15 * w_ref[1, z]
        coef[0, z] = jnp.where(row == 127, 0.0, 0.15 + wx)
        coef[1, z] = jnp.where(row == 0, 0.0, 0.15 - wx)
        coef[2, z] = jnp.where(lane == 127, 0.0, 0.15 + wy)
        coef[3, z] = jnp.where(lane == 0, 0.0, 0.15 - wy)
        below = 0.15 + 0.15 * w_ref[2, jnp.maximum(z - 1, 0)]
        above = 0.15 - 0.15 * w_ref[2, jnp.minimum(z + 1, 3)]
        coef[4, z] = jnp.where(z > 0, below, 0.0)
        coef[5, z] = jnp.where(z < 3, above, 0.0)
        coef[6, z] = jnp.where(lane == 0, 0.15 - wy, 0.15 + wy)
        return carry

    lax.fori_loop(0, 4, make_coef, 0)
    fetches[1].wait()
    fetches[6].wait()

    def pack(src, items, send_x, send_y):
        packed = jnp.zeros((128, 128), F32)
        for k, (v, z) in enumerate(items):
            last = (0.15 + 0.15 * w_ref[0, z, 120:128, :]) * src[v, z, 120:128, :]
            first = (0.15 - 0.15 * w_ref[0, z, 0:8, :]) * src[v, z, 0:8, :]
            send_x[0, k : k + 1, :] = last[7:8, :]
            send_x[1, k : k + 1, :] = first[0:1, :]
            rolled = pltpu.roll(coef[6, z] * src[v, z], 2 * k + 1, 1)
            packed = jnp.where((lane == 2 * k) | (lane == 2 * k + 1), rolled, packed)
        send_y[...] = packed.T[0 : send_y.shape[0], :]

    def send_edges(at, send_x, send_y, recv_x, recv_y):
        for side, target in ((0, (up_a, b)), (1, (down_a, b))):
            remote(
                send_x.at[side],
                recv_x.at[side],
                edge_sems.at[0, at, side],
                edge_sems.at[1, at, side],
                target,
            )
        for side, target in ((0, (a, up_b)), (1, (a, down_b))):
            remote(
                send_y,
                recv_y.at[side],
                edge_sems.at[0, at, 2 + side],
                edge_sems.at[1, at, 2 + side],
                target,
            )

    def wait_edges(at, recv_x, recv_y):
        for side in range(2):
            take(recv_x.at[side], edge_sems.at[1, at, side])
            take(recv_y.at[side], edge_sems.at[1, at, 2 + side])
        rows = recv_y.shape[1]
        odd = (iota((rows, 128), 0) & 1) == 1
        up = jnp.where(b > 0, recv_y[0], 0.0)
        down = jnp.where(b < nb - 1, recv_y[1], 0.0)
        mixed = jnp.where(odd, pltpu.roll(up, 1, 0), pltpu.roll(down, rows - 1, 0))
        if rows < 128:
            mixed = jnp.concatenate([mixed, jnp.zeros((128 - rows, 128), F32)], axis=0)
        turned[...] = mixed.T

    def drain_edges(at, send_x, send_y):
        for side in range(2):
            take(send_x.at[side], edge_sems.at[0, at, side])
            take(send_y, edge_sems.at[0, at, 2 + side])

    def mend(dst, recv_x, k, v, z):
        rolled = pltpu.roll(turned[...], 127 - 2 * k, 1)
        whole = dst[v, z] + jnp.where((lane == 0) | (lane == 127), rolled, 0.0)
        from_down = jnp.where(a > 0, recv_x[0, k : k + 1, :], 0.0)
        from_up = jnp.where(a < na - 1, recv_x[1, k : k + 1, :], 0.0)
        dst[v, z, 8:120, :] = whole[8:120]
        dst[v, z, 0:8, :] = whole[0:8] + jnp.where(row8 == 0, from_down, 0.0)
        dst[v, z, 120:128, :] = whole[120:128] + jnp.where(row8 == 7, from_up, 0.0)

    def advance(src, dst, v, z):
        u = src[v, z]
        total = mix_ref[v, 0] * src[0, z]
        for w in range(1, 8):
            total = total + mix_ref[v, w] * src[w, z]
        total = 0.3 * total + 0.1 * u
        total = total + pltpu.roll(coef[0, z] * u, 1, 0) + pltpu.roll(coef[1, z] * u, 127, 0)
        total = total + pltpu.roll(coef[2, z] * u, 1, 1) + pltpu.roll(coef[3, z] * u, 127, 1)
        if not (isinstance(z, int) and z == 0):
            total = total + coef[4, z] * src[v, z - 1 if isinstance(z, int) else jnp.maximum(z - 1, 0)]
        if not (isinstance(z, int) and z == 3):
            total = total + coef[5, z] * src[v, z + 1 if isinstance(z, int) else jnp.minimum(z + 1, 3)]
        dst[v, z] = total

    def advance_all(src, dst, vs, z):
        def one(v, carry):
            advance(src, dst, v, z)
            return carry

        lax.fori_loop(0, vs, one, 0)

    near = [(v, z) for z in (0, 1) for v in range(8)] + [(7, 2)]
    far = [(v, 2) for v in range(7)] + [(v, 3) for v in range(8)]
    faced = [(7, 0), (7, 1)]
    later = [(v, z) for z in range(4) for v in range(8) if (v, z) not in faced]
    first = (first_send_x, first_send_y, first_recv_x, first_recv_y)
    rest = (rest_send_x, rest_send_y, rest_recv_x, rest_recv_y)
    of_faces = (face_send_x, face_send_y, face_recv_x, face_recv_y)
    last = (last_send_x, last_send_y, last_recv_x, last_recv_y)

    pack(u_ref, near, first_send_x, first_send_y)
    at_0, at_1 = near.index((7, 0)), near.index((7, 1))
    for side in range(2):
        for z, k in enumerate((at_0, at_1)):
            corner_send[2 * side + z : 2 * side + z + 1, :] = first_send_x[side, k : k + 1, :]
            corner_send[4 + 2 * side + z : 5 + 2 * side + z, :] = first_send_y[
                2 * k + side : 2 * k + side + 1, :
            ]
    pl.semaphore_wait(barrier, len(greeted))
    send_edges(0, *first)
    for at, target in enumerate(corners):
        remote(corner_send, corner_recv.at[at], corner_sems.at[0, at], corner_sems.at[1, at], target)
    for move in y_moves:
        signal(ready.at[0], device(move))

    for z in (0, 1):
        advance(u_ref, u1, 7, z)
    columns = jnp.zeros((128, 128), F32)
    for z in (0, 1):
        upper = 0.15 + 0.15 * w_ref[0, z, 120:128, :]
        lower = 0.15 - 0.15 * w_ref[0, z, 0:8, :]
        face_send_x[0, z : z + 1, :] = (upper * u1[7, z, 120:128, :])[7:8, :]
        face_send_x[0, 2 + z : 3 + z, :] = upper[7:8, :]
        face_send_x[1, z : z + 1, :] = (lower * u1[7, z, 0:8, :])[0:1, :]
        face_send_x[1, 2 + z : 3 + z, :] = lower[0:1, :]
        factor = coef[6, z]
        scaled = factor * u1[7, z]
        columns = jnp.where(lane == z, pltpu.roll(scaled, 1 + z, 1), columns)
        columns = jnp.where(lane == 2 + z, pltpu.roll(factor, 3 + z, 1), columns)
        columns = jnp.where(lane == 4 + z, pltpu.roll(scaled, 4 + z, 1), columns)
        columns = jnp.where(lane == 6 + z, pltpu.roll(factor, 6 + z, 1), columns)
    face_send_y[...] = columns.T[0:8, :]
    send_edges(1, *of_faces)
    for z in (0, 1):
        advance_all(u_ref, u1, 7, z)
    advance(u_ref, u1, 7, 2)
    if y_moves:
        pl.semaphore_wait(ready.at[0], len(y_moves))
    for move in blk_moves:
        signal(ready.at[1], device(move))

    owner = jnp.broadcast_to(owner_ref[...].astype(F32), (128, 256)).T.astype(I32)
    owner_hot = jnp.where(iota((256, 128), 1) == owner, 1.0, 0.0)
    earlier = jnp.where(iota((256, 256), 0) > iota((256, 256), 1), 1.0, 0.0).astype(BF16)
    before = dot(earlier, owner_hot.astype(BF16))
    rank = jnp.sum(before * owner_hot, axis=1, keepdims=True)
    slot = owner.astype(F32) * float(cap) + rank
    slot_row = slot.T[0:1, :]
    sel = jnp.where(iota((slots, 256), 0).astype(F32) == slot_row, 1.0, 0.0).astype(BF16)
    flip = jnp.where(iota((256, 256), 0) == (iota((256, 256), 1) ^ 7), 1.0, 0.0).astype(BF16)
    sel_t[...] = dot(sel, flip).astype(BF16)
    tile_high, tile_low = split(jnp.broadcast_to(tile_ref[...].astype(F32), (128, 256)).T)
    label_ref[...] = dot(sel, tile_high) + dot(sel, tile_low)
    pack(u_ref, far, rest_send_x, rest_send_y)
    send_edges(2, *rest)

    wait_edges(0, first_recv_x, first_recv_y)
    for k, (v, z) in enumerate(near):
        mend(u1, first_recv_x, k, v, z)
    for z in (0, 1):
        advance(u1, out_ref, 7, z)

    for side in range(2):
        take(face_recv_x.at[side], edge_sems.at[1, 1, side])
        take(face_recv_y.at[side], edge_sems.at[1, 1, 2 + side])
    for at in range(4):
        take(corner_recv.at[at], corner_sems.at[1, at])
    own = corner_send[...]
    low_low = jnp.where((a > 0) & (b > 0), corner_recv[0], 0.0)
    low_high = jnp.where((a > 0) & (b < nb - 1), corner_recv[1], 0.0)
    high_low = jnp.where((a < na - 1) & (b > 0), corner_recv[2], 0.0)
    high_high = jnp.where((a < na - 1) & (b < nb - 1), corner_recv[3], 0.0)
    low_low, high_high = pltpu.roll(low_low, 1, 1), pltpu.roll(high_high, 127, 1)
    lane2 = iota((2, 128), 1)

    def beyond(came, rows, first_rows, last_rows):
        brought = rows + jnp.where(lane2 == 0, first_rows, 0.0)
        brought = brought + jnp.where(lane2 == 127, last_rows, 0.0)
        return came[0:2] + came[2:4] * brought

    from_left = beyond(face_recv_y[0, 0:4], own[6:8], low_low[0:2], high_low[2:4])
    from_right = beyond(face_recv_y[1, 4:8], own[4:6], low_high[0:2], high_high[2:4])
    from_left = jnp.where(b > 0, from_left, 0.0)
    from_right = jnp.where(b < nb - 1, from_right, 0.0)
    ring_x[0, 0:2, :] = beyond(face_recv_x[0, 0:4], own[2:4], low_low[4:6], low_high[6:8])
    ring_x[1, 0:2, :] = beyond(face_recv_x[1, 0:4], own[0:2], high_low[4:6], high_high[6:8])
    beside = [from_right[0:1], from_left[0:1], from_right[1:2], from_left[1:2]]
    turned[...] = jnp.concatenate(beside + [jnp.zeros((124, 128), F32)], axis=0).T
    for k, (v, z) in enumerate(faced):
        mend(out_ref, ring_x, k, v, z)
    current = out_ref[7, 1] - out_ref[7, 0]

    halves = [pltpu.roll(current, 64, 1).reshape(16, 8, 128), current.reshape(16, 8, 128)]
    group = iota((16, 8, 128), 2) // 8
    faces = []
    for half in range(2):
        face = jnp.zeros((16, 8, 128), F32)
        for r in range(8):
            spread = jnp.broadcast_to(halves[half][:, r : r + 1, :], (16, 8, 128))
            moved = pltpu.roll(spread, 8 * r + 8, 2, stride=8, stride_axis=1)
            face = jnp.where(group == r, moved, face)
        faces.append(face)
    faces = jnp.stack(faces, axis=1).reshape(256, 128)
    face_high, face_low = split(faces)
    routed = dot(sel_t[...], face_high) + dot(sel_t[...], face_low)
    lane_slot = iota((slots, 128), 1)
    routed = jnp.where(lane_slot < 64, routed, label_ref[...])
    face_send[...] = routed.reshape(count, cap, 128)

    def send_all(src, dst, at):
        for move in moves:
            peer_of_a, peer_of_b = device(move)
            remote(
                src.at[peer_of_a * nb + peer_of_b],
                dst.at[me],
                send_sems.at[at],
                recv_sems.at[at],
                (peer_of_a, peer_of_b),
            )
        dst[me] = src[me]

    pl.semaphore_wait(ready.at[1], len(blk_moves))
    send_all(face_send, face_recv, 0)

    advance_all(u_ref, u1, 7, 2)
    advance_all(u_ref, u1, 8, 3)
    wait_edges(2, rest_recv_x, rest_recv_y)
    for k, (v, z) in enumerate(far):
        mend(u1, rest_recv_x, k, v, z)
    pack(u1, later, last_send_x, last_send_y)
    send_edges(3, *last)

    fetches[2].wait()
    fetches[3].wait()

    def per_row(column):
        return jnp.sum(
            jnp.where(iota((orders, 128), 1) == column, twiddle_ref[...], 0.0),
            axis=1,
            keepdims=True,
        )

    def rows_of(even, odd):
        return jnp.concatenate([even, odd], axis=2).reshape(spec_rows, lon)

    def waves():
        cos_turn, sin_turn = per_row(b), per_row(b + 32)
        cos_wave, sin_wave = wave_ref[0], wave_ref[1]
        cosine = (cos_turn * cos_wave - sin_turn * sin_wave).reshape(nb, 2, 1, PAIRS, lon)
        sine = (sin_turn * cos_wave + cos_turn * sin_wave).reshape(nb, 2, 1, PAIRS, lon)
        return cosine, sine

    cosine, sine = waves()
    base_high, base_low = split(rows_of(cosine, sine) * (1.0 / cols_total))
    base_ref[0] = base_high
    base_ref[1] = base_low

    take(face_recv.at[pl.ds(0, count - 1)], recv_sems.at[0])
    got = face_recv[...].reshape(slots, 128)
    swapped = pltpu.roll(got, 64, 1)
    label = jnp.where(lane_slot < 64, swapped, got).astype(I32)
    face = jnp.where(lane_slot < 64, got, swapped)
    tile_row, tile_col = label >> 5, label & 31
    tile_row_t = tile_row.astype(F32).T.astype(I32)
    scatter = jnp.where(iota((32, slots), 0) == tile_row_t[0:32, :], 1.0, 0.0).astype(BF16)
    scatter = jnp.concatenate([scatter, scatter], axis=1)
    col_masks = [
        jnp.where((lane_slot >> 3) + 16 * half == tile_col, 1.0, 0.0).astype(BF16)
        for half in range(2)
    ]

    def spread_bit(value, width):
        moved = pltpu.roll(value, width, 1)
        bit = (lane_slot & width) == 0
        return [jnp.where(bit, value, moved), jnp.where(bit, moved, value)]

    lines = [face]
    for width in (32, 16, 8):
        lines = [part for line in lines for part in spread_bit(line, width)]
    for r in range(8):
        line_high, line_low = split(lines[r])
        right = jnp.concatenate(
            [
                jnp.concatenate([part * mask for mask in col_masks], axis=1)
                for part in (line_high, line_low)
            ],
            axis=0,
        )
        rows = dot(scatter, right)
        forcing[0, pl.ds(r, 32, stride=8), :] = rows[:, 0:128]
        forcing[1, pl.ds(r, 32, stride=8), :] = rows[:, 128:256]

    force = split(jnp.concatenate([forcing[0], forcing[1]], axis=1))
    spectrum = dot3((base_ref[0], base_ref[1]), force, ((1,), (1,)))
    spec_send[...] = spectrum.reshape(nb, 4 * PAIRS, lat)
    for move in inner_moves:
        peer = peer_b[move[2:]]
        remote(spec_send.at[peer], spec_recv.at[b], send_sems.at[1], recv_sems.at[1], (a, peer))
    spec_recv[b] = spec_send[b]

    fetches[4].wait()
    row_of_lane = a * lat + iota((PAIRS, lat), 1)
    x = -1.0 + (2.0 * row_of_lane.astype(F32) + 1.0) / rows_total
    log_sine = jnp.log(jnp.sqrt(1.0 - x * x))
    turns = steps // 16
    heads = ratios[turns]
    low_start = jnp.exp(heads[:, 1:2] + heads[:, 0:1] * log_sine)
    high_start = jnp.exp(heads[:, 3:4] + heads[:, 2:3] * log_sine)

    def build(turn, carry):
        previous, older = carry
        block = ratios[turn]
        made = []
        for offset in range(16):
            up = block[:, offset : offset + 1]
            down = block[:, 16 + offset : 17 + offset]
            begin_low = block[:, 32 + offset : 33 + offset]
            begin_high = block[:, 48 + offset : 49 + offset]
            present = (
                begin_low * low_start + begin_high * high_start + up * x * previous - down * older
            )
            made.append(present)
            older, previous = previous, present
        where = pl.ds(pl.multiple_of(turn * 128, 128), 128)
        for at, part in enumerate(split3(jnp.concatenate(made, axis=0))):
            leg[at, where, :] = part
        return previous, older

    empty = jnp.zeros((PAIRS, lat), F32)
    lax.fori_loop(0, turns, build, (empty, empty))

    width = steps * PAIRS
    at_step = iota((PAIRS, width), 1) // PAIRS
    at_pair = lax.rem(iota((PAIRS, width), 1), PAIRS)
    order_low = b * PAIRS + at_pair
    is_high = at_step <= order_low
    degree = jnp.where(is_high, orders - 1 - order_low + at_step, at_step - 1).astype(F32)
    scale = (2.0 / rows_total) * GAIN / (degree * (degree + 1.0) + SCREENING)
    scale = jnp.where(at_step <= orders, scale, 0.0)
    mine = at_pair == iota((PAIRS, width), 0)
    mask_ref[0] = jnp.where(mine & jnp.logical_not(is_high), scale, 0.0)
    mask_ref[1] = jnp.where(mine & is_high, scale, 0.0)

    order_col, weight_col = per_row(64), per_row(65)
    cosine, sine = waves()
    weight = weight_col.reshape(nb, 2, 1, PAIRS, 1)
    slope_weight = (weight_col * order_col).reshape(nb, 2, 1, PAIRS, 1)
    value_high, value_low = split(rows_of(cosine * weight, sine * weight))
    values_ref[0, :, 0:lon] = value_high
    values_ref[1, :, 0:lon] = value_low
    slope_high, slope_low = split(rows_of(-sine * slope_weight, cosine * slope_weight))
    values_ref[0, :, lon : 2 * lon] = slope_high
    values_ref[1, :, lon : 2 * lon] = slope_low

    take(spec_recv.at[pl.ds(0, nb - 1)], recv_sems.at[1])
    spec = spec_recv[0]
    for at in range(1, nb):
        spec = spec + spec_recv[at]
    spec_high, spec_low = split(spec)
    both = dot(jnp.concatenate([spec_high, spec_low], axis=0), leg[0], ((1,), (1,)))
    wide_sums = both[0:32] + both[32:64] + dot(spec_high, leg[1], ((1,), (1,)))
    for parity in range(2):
        low_rows = wide_sums[parity * 8 : parity * 8 + 8]
        high_rows = wide_sums[16 + parity * 8 : 24 + parity * 8]
        kept = low_rows * mask_ref[0] + high_rows * mask_ref[1]
        coef_send[parity : parity + 1, :] = jnp.sum(kept, axis=0, keepdims=True)
    for move in blk_moves:
        remote(
            coef_send,
            coef_recv.at[a],
            send_sems.at[2],
            recv_sems.at[2],
            (peer_a[move[:2]], b),
        )
    coef_recv[a] = coef_send[...]
    for z in (0, 1):
        advance_all(u1, out_ref, 7, z)
    take(coef_recv.at[pl.ds(0, na - 1)], recv_sems.at[2])
    solved = coef_recv[0]
    for at in range(1, na):
        solved = solved + coef_recv[at]
    expanded = []
    for kind in range(2):
        for parity in range(2):
            expanded.append(
                jnp.where(
                    mask_ref[kind] != 0.0,
                    jnp.broadcast_to(solved[parity : parity + 1, :], (PAIRS, width)),
                    0.0,
                )
            )
    solved_high, solved_low = split(jnp.concatenate(expanded, axis=0))
    solved_both = jnp.concatenate([solved_high, solved_low], axis=0)
    fine = dot(solved_high, leg[2])
    both = dot(solved_both, leg[0])
    middle = dot(solved_both, leg[1])
    syn_all[b] = both[0:32] + (both[32:64] + (middle[0:32] + (middle[32:64] + fine)))
    for move in inner_moves:
        remote(
            syn_all.at[b],
            syn_all.at[b],
            send_sems.at[3],
            recv_sems.at[3],
            (a, peer_b[move[2:]]),
        )
    for z in (2, 3):
        advance_all(u1, out_ref, 8, z)
    wait_edges(3, last_recv_x, last_recv_y)
    for k, (v, z) in enumerate(later):
        mend(out_ref, last_recv_x, k, v, z)
    take(syn_all.at[pl.ds(0, nb - 1)], recv_sems.at[3])

    syn_high, syn_middle, syn_low = split3(syn_all[...].reshape(spec_rows, lat).T)

    def potential_of(high, middle, low):
        rows = high.shape[0]
        coarse = dot(jnp.concatenate([high, middle, low], axis=0), values_ref[0, :, 0:lon])
        rest_of = dot(jnp.concatenate([high, middle], axis=0), values_ref[1, :, 0:lon])
        return coarse[0:rows] + (
            coarse[rows : 2 * rows] + (rest_of[0:rows] + (coarse[2 * rows :] + rest_of[rows:]))
        )

    def rims_of(part):
        return jnp.concatenate([part[0:16], part[lat - 16 :]], axis=0)

    rims = potential_of(rims_of(syn_high), rims_of(syn_middle), rims_of(syn_low))
    rim_send[0] = rims[0:8]
    rim_send[1] = rims[24:32]
    remote(rim_send.at[1], rim_recv.at[0], rim_sems.at[0, 0], rim_sems.at[1, 0], (up_a, b))
    remote(rim_send.at[0], rim_recv.at[1], rim_sems.at[0, 1], rim_sems.at[1, 1], (down_a, b))
    potential = potential_of(syn_high, syn_middle, syn_low)
    pot_ref[...] = potential
    turned_slopes = dot(
        jnp.concatenate([syn_high, syn_middle], axis=0), values_ref[0, :, lon : 2 * lon]
    )
    azimuthal = turned_slopes[0:lat] + (
        turned_slopes[lat:] + dot(syn_high, values_ref[1, :, lon : 2 * lon])
    )
    fetches[5].wait()
    grid_row = iota((lat, 1), 0)
    global_row = a * lat + grid_row
    x_col = -1.0 + (2.0 * global_row.astype(F32) + 1.0) / rows_total
    sine_col = jnp.sqrt(1.0 - x_col * x_col)
    eastward = azimuthal / sine_col
    inverse = rows_total / 2.0

    def heat_of(first_row, last_row, above, below):
        part = slice(first_row, last_row)
        at_first, at_last = global_row[part] == 0, global_row[part] == rows_total - 1
        here = potential[part]
        slope = (jnp.where(at_last, here, above) - jnp.where(at_first, here, below)) * (
            jnp.where(at_first | at_last, inverse, 0.5 * inverse)
        )
        polar = sine_col[part] * slope
        return ped_ref[part, :] * (polar * polar + eastward[part] * eastward[part])

    above, below = pltpu.roll(potential, lat - 1, 0), pltpu.roll(potential, 1, 0)
    heating = heat_of(0, lat, above, below)
    heat_ref[...] = heating

    grids[0] = potential[:, 0:128]
    grids[1] = potential[:, 128:256]
    grids[2] = heating[:, 0:128]
    grids[3] = heating[:, 128:256]
    pick = iota((slots, 128), 1)
    pick = jnp.where((pick < 96) & ((pick & 31) == tile_row), 1.0, 0.0).astype(BF16)
    bits = [(tile_col & (1 << at)) != 0 for at in range(5)]
    upper = lane_slot >= 64

    def pick_row(r):
        rows = jnp.concatenate([grids[at, pl.ds(r, 32, stride=8), :] for at in range(4)], axis=1)
        high, middle, low = split3(rows)
        parts = jnp.concatenate([high, middle, low, jnp.zeros_like(low)], axis=0)
        picked = dot(pick, parts)
        pot = jnp.where(bits[4], picked[:, 128:256], picked[:, 0:128])
        heat = jnp.where(bits[4], picked[:, 384:512], picked[:, 256:384])
        wide[r] = jnp.where(
            upper,
            jnp.where(bits[3], heat, pltpu.roll(heat, 64, 1)),
            jnp.where(bits[3], pltpu.roll(pot, 64, 1), pot),
        )

    for r in range(1, 7):
        pick_row(r)
    take(rim_recv.at[0], rim_sems.at[1, 0])
    take(rim_recv.at[1], rim_sems.at[1, 1])
    edge8 = iota((8, lon), 0)
    top = heat_of(0, 8, above[0:8], jnp.where(edge8 == 0, rim_recv[0, 7:8, :], below[0:8]))
    bottom = heat_of(
        lat - 8, lat, jnp.where(edge8 == 7, rim_recv[1, 0:1, :], above[lat - 8 :]), below[lat - 8 :]
    )
    for first_row, part in ((0, top), (lat - 8, bottom)):
        heat_ref[first_row : first_row + 8, :] = part
        grids[2, first_row : first_row + 8, :] = part[:, 0:128]
        grids[3, first_row : first_row + 8, :] = part[:, 128:256]
    for r in (0, 7):
        pick_row(r)

    def join(first, second, at):
        width = 8 << at
        return jnp.where(
            (lane_slot & width) == 0,
            jnp.where(bits[at], pltpu.roll(first, 128 - width, 1), first),
            jnp.where(bits[at], second, pltpu.roll(second, width, 1)),
        )

    quads = [join(wide[r], wide[r + 4], 2) for r in range(4)]
    twos = [join(quads[r], quads[r + 2], 1) for r in range(2)]
    reply_send[...] = join(twos[0], twos[1], 0).reshape(count, cap, 128)
    send_all(reply_send, reply_recv, 4)
    chosen = jnp.where(iota((256, slots), 1).astype(F32) == slot[:, 0:1], 1.0, 0.0).astype(BF16)
    take(reply_recv.at[pl.ds(0, count - 1)], recv_sems.at[4])
    back_high, back_low = split(reply_recv[...].reshape(slots, 128))
    blocks_ref[...] = dot(chosen, back_high) + dot(chosen, back_low)

    for at, (sent_x, sent_y, _, _) in enumerate((first, of_faces, rest, last)):
        drain_edges(at, sent_x, sent_y)
    take(face_send.at[pl.ds(0, count - 1)], send_sems.at[0])
    take(spec_send.at[pl.ds(0, nb - 1)], send_sems.at[1])
    take(coef_recv.at[pl.ds(0, na - 1)], send_sems.at[2])
    take(syn_all.at[pl.ds(0, nb - 1)], send_sems.at[3])
    take(reply_send.at[pl.ds(0, count - 1)], send_sems.at[4])
    for at in range(4):
        take(corner_send, corner_sems.at[0, at])
    take(rim_send.at[0], rim_sems.at[0, 1])
    take(rim_send.at[1], rim_sems.at[0, 0])


def write_out(slab, potential, heating, blocks, *refs):
    pieces = [(slab.at[v], refs[0].at[v]) for v in range(8)]
    pieces += [(potential, refs[1]), (heating, refs[2]), (blocks, refs[3])]
    copies = [
        pltpu.make_async_copy(src, dst, refs[4].at[k]) for k, (src, dst) in enumerate(pieces)
    ]
    for copy in copies:
        copy.start()
    for copy in copies:
        copy.wait()


def solution(mesh):
    na, nb = mesh.shape["blk"], mesh.shape["inner"]
    count = na * nb

    def shards(slab, speeds, source_matrix, pedersen, owners, tile_positions):
        lat, lon = pedersen.shape
        blocks = owners.shape[0]
        cap = max(2, 2 * blocks // count)
        slots = count * cap
        orders = PAIRS * 2 * nb
        wave, twiddle, table, steps = spectral_tables(na, nb, lat, lon)
        width = steps * PAIRS
        vmem = pl.BlockSpec(memory_space=pltpu.VMEM)
        hbm = pl.BlockSpec(memory_space=pl.ANY)
        dma = pltpu.SemaphoreType.DMA
        shapes = (slab.shape, (lat, lon), (lat, lon), (blocks, 128))

        def edges(rows_x, rows_y):
            return [
                pltpu.VMEM((2, rows_x, 128), F32),
                pltpu.VMEM((rows_y, 128), F32),
                pltpu.VMEM((2, rows_x, 128), F32),
                pltpu.VMEM((2, rows_y, 128), F32),
            ]

        results = pl.pallas_call(
            functools.partial(kernel, (na, nb, steps)),
            out_shape=tuple(pltpu.VMEM(shape, F32) for shape in shapes),
            in_specs=[
                hbm,
                hbm,
                pl.BlockSpec(memory_space=pltpu.SMEM),
                hbm,
                vmem,
                vmem,
                hbm,
                hbm,
                hbm,
            ],
            out_specs=(vmem,) * 4,
            scratch_shapes=[
                pltpu.VMEM(slab.shape, F32),
                pltpu.VMEM(speeds.shape, F32),
                pltpu.VMEM((lat, lon), F32),
                pltpu.VMEM(wave.shape, F32),
                pltpu.VMEM(twiddle.shape, F32),
                pltpu.VMEM((steps // 16 + 1, PAIRS, 128), F32),
                pltpu.VMEM((7, 4, 128, 128), F32),
                pltpu.VMEM((8, 4, 128, 128), F32),
                *edges(24, 40),
                *edges(16, 32),
                *edges(8, 8),
                pltpu.VMEM((2, 8, 128), F32),
                pltpu.VMEM((8, 128), F32),
                pltpu.VMEM((4, 8, 128), F32),
                *edges(32, 64),
                pltpu.VMEM((128, 128), F32),
                pltpu.VMEM((slots, 256), BF16),
                pltpu.VMEM((slots, 128), F32),
                pltpu.VMEM((count, cap, 128), F32),
                pltpu.VMEM((count, cap, 128), F32),
                pltpu.VMEM((2, lat, 128), F32),
                pltpu.VMEM((2, 2 * orders, lon), BF16),
                pltpu.VMEM((2, 2 * orders, 2 * lon), BF16),
                pltpu.VMEM((nb, 4 * PAIRS, lat), F32),
                pltpu.VMEM((nb, 4 * PAIRS, lat), F32),
                pltpu.VMEM((3, width, lat), BF16),
                pltpu.VMEM((2, PAIRS, width), F32),
                pltpu.VMEM((2, width), F32),
                pltpu.VMEM((na, 2, width), F32),
                pltpu.VMEM((nb, 4 * PAIRS, lat), F32),
                pltpu.VMEM((2, 8, lon), F32),
                pltpu.VMEM((2, 8, lon), F32),
                pltpu.VMEM((4, lat, 128), F32),
                pltpu.VMEM((8, slots, 128), F32),
                pltpu.VMEM((count, cap, 128), F32),
                pltpu.VMEM((count, cap, 128), F32),
                dma((2, 4, 4)),
                dma((5,)),
                dma((5,)),
                dma((2, 2)),
                dma((2, 4)),
                dma((7,)),
                pltpu.SemaphoreType.REGULAR((2,)),
            ],
            compiler_params=pltpu.CompilerParams(
                collective_id=0, has_side_effects=True, vmem_limit_bytes=VMEM_LIMIT
            ),
        )(
            slab,
            speeds,
            source_matrix,
            pedersen,
            owners.reshape(1, blocks),
            tile_positions.reshape(1, blocks),
            jnp.asarray(wave),
            jnp.asarray(twiddle),
            jnp.asarray(table),
        )
        return pl.pallas_call(
            write_out,
            out_shape=tuple(jax.ShapeDtypeStruct(shape, F32) for shape in shapes),
            in_specs=[vmem] * 4,
            out_specs=(hbm,) * 4,
            scratch_shapes=[dma((11,))],
            compiler_params=pltpu.CompilerParams(vmem_limit_bytes=16 * 1024 * 1024),
        )(*results)

    in_specs = (
        P(None, None, "blk", "inner"),
        P(None, None, "blk", "inner"),
        P(),
        P("blk", "inner"),
        P(("blk", "inner"), None),
        P(("blk", "inner")),
    )
    out_specs = (
        P(None, None, "blk", "inner"),
        P("blk", "inner"),
        P("blk", "inner"),
        P(("blk", "inner"), None),
    )
    return jax.shard_map(shards, mesh=mesh, in_specs=in_specs, out_specs=out_specs, check_vma=False)
```

profile of v0, /device:TPU:1, one launch (start us, length us, event | category | flops | bytes accessed | tf_op | source)
XLA Modules:
  0.0 60.8 jit_solution(13287499585875468979)
XLA Ops:
  0.6 58.4 %shard_map.120 = (f32[8,4,128,128]{3,2,1,0:T(8,128)S(1)}, f32[256,256]{1,0:T(8,128)S(1)}, f32[256,256]{1,0:T(8,128)S(1)}, f32[256,128]{1,0:T(8,128)S(1)}) custom-call(f32[8,4,128,128]{3,2,1,0:T(8,128)} %u_hbm.1, f32[3,4,128,128]{3,2,1,0:T(8,128)} %w_hbm.1, f32[8,8]{1,0:T(8,128)} %mix_ref.1, f32[256,256]{1,0:T(8,128)} %ped_hbm.1, s32[1,256]{1,0:T(1,128)} %bitcast.2, ...), custom_call_target="tpu_custom_call" | custom-call | tf_op jit(solution)/shard_map/pallas_call | solution.py:829
  59.0 1.6 %shard_map.121 = (f32[8,4,128,128]{3,2,1,0:T(8,128)}, f32[256,256]{1,0:T(8,128)}, f32[256,256]{1,0:T(8,128)}, f32[256,128]{1,0:T(8,128)}) custom-call(f32[8,4,128,128]{3,2,1,0:T(8,128)S(1)} %get-tuple-element.8.slab, f32[256,256]{1,0:T(8,128)S(1)} %get-tuple-element.9.potential, f32[256,256]{1,0:T(8,128)S(1)} %get-tuple-element.10.heating, ...), custom_call_target="tpu_custom_call" | custom-call | tf_op jit(solution)/shard_map/pallas_call | solution.py:903
where the time goes:
time: 61 us; the launch traced here: 60.8 us
  Pallas kernels  60 us (98%)
  between operations  0.8 us (1%)
    pallas_call x1, Pallas kernels, shards(): pl.pallas_call(functools.partial(kernel, (na, nb, steps)), out_shape=tupl...  58.4 us
    pallas_call x1, Pallas kernels, shards(): pl.pallas_call(write_out, out_shape=tuple((jax.ShapeDtypeStruct(shape, F3...  1.62 us

commit v1 on v0

--- a/solution.py
+++ b/solution.py
@@ -120,6 +120,8 @@
     ratios,
     coef,
     u1,
+    q_ref,
+    source_ref,
     first_send_x,
     first_send_y,
     first_recv_x,
@@ -227,6 +229,23 @@
     up_a, down_a = lax.rem(a + 1, na), lax.rem(a + na - 1, na)
     up_b, down_b = lax.rem(b + 1, nb), lax.rem(b + nb - 1, nb)
 
+    fetches = [
+        pltpu.make_async_copy(src, dst, in_sems.at[at])
+        for at, (src, dst) in enumerate(
+            [
+                (w_hbm, w_ref),
+                (u_hbm.at[7], u_ref.at[7]),
+                (u_hbm.at[pl.ds(0, 7), pl.ds(0, 3)], u_ref.at[pl.ds(0, 7), pl.ds(0, 3)]),
+                (u_hbm.at[pl.ds(0, 7), pl.ds(3, 1)], u_ref.at[pl.ds(0, 7), pl.ds(3, 1)]),
+                (twiddle_hbm, twiddle_ref),
+                (wave_hbm, wave_ref),
+                (table_hbm.at[b], ratios),
+                (ped_hbm, ped_ref),
+            ]
+        )
+    ]
+    for fetch in fetches:
+        fetch.start()
     barrier = pltpu.get_barrier_semaphore()
     y_moves = [move for move in inner_moves if move[3] == 0]
     z_moves = [move for move in inner_moves if move[2] == 0]
@@ -236,22 +255,6 @@
     greeted += corners
     for target in greeted:
         signal(barrier, target)
-    fetches = [
-        pltpu.make_async_copy(src, dst, in_sems.at[at])
-        for at, (src, dst) in enumerate(
-            [
-                (w_hbm, w_ref),
-                (u_hbm.at[:, pl.ds(0, 2)], u_ref.at[:, pl.ds(0, 2)]),
-                (twiddle_hbm, twiddle_ref),
-                (wave_hbm, wave_ref),
-                (table_hbm.at[b], ratios),
-                (ped_hbm, ped_ref),
-                (u_hbm.at[:, pl.ds(2, 2)], u_ref.at[:, pl.ds(2, 2)]),
-            ]
-        )
-    ]
-    for at in (0, 1, 6, 2, 3, 4, 5):
-        fetches[at].start()
 
     row = iota((128, 128), 0)
     lane = iota((128, 128), 1)
@@ -272,17 +275,34 @@
         return carry
 
     lax.fori_loop(0, 4, make_coef, 0)
+
+    def weighted(weights, z):
+        total = weights[0] * u_ref[0, z]
+        for w in range(1, 8):
+            total = total + weights[w] * u_ref[w, z]
+        return total
+
+    source = [mix_ref[7, w] for w in range(8)]
+    second = []
+    for w in range(8):
+        total = source[0] * mix_ref[0, w]
+        for k in range(1, 8):
+            total = total + source[k] * mix_ref[k, w]
+        second.append(total)
     fetches[1].wait()
-    fetches[6].wait()
+    fetches[2].wait()
+    for z in range(3):
+        q_ref[z] = weighted(source, z)
 
     def pack(src, items, send_x, send_y):
         packed = jnp.zeros((128, 128), F32)
         for k, (v, z) in enumerate(items):
-            last = (0.15 + 0.15 * w_ref[0, z, 120:128, :]) * src[v, z, 120:128, :]
-            first = (0.15 - 0.15 * w_ref[0, z, 0:8, :]) * src[v, z, 0:8, :]
+            cells = q_ref.at[z] if v == 8 else src.at[v, z]
+            last = (0.15 + 0.15 * w_ref[0, z, 120:128, :]) * cells[120:128, :]
+            first = (0.15 - 0.15 * w_ref[0, z, 0:8, :]) * cells[0:8, :]
             send_x[0, k : k + 1, :] = last[7:8, :]
             send_x[1, k : k + 1, :] = first[0:1, :]
-            rolled = pltpu.roll(coef[6, z] * src[v, z], 2 * k + 1, 1)
+            rolled = pltpu.roll(coef[6, z] * cells[...], 2 * k + 1, 1)
             packed = jnp.where((lane == 2 * k) | (lane == 2 * k + 1), rolled, packed)
         send_y[...] = packed.T[0 : send_y.shape[0], :]
 
@@ -322,14 +342,24 @@
             take(send_x.at[side], edge_sems.at[0, at, side])
             take(send_y, edge_sems.at[0, at, 2 + side])
 
-    def mend(dst, recv_x, k, v, z):
+    def mend(cells, recv_x, k):
         rolled = pltpu.roll(turned[...], 127 - 2 * k, 1)
-        whole = dst[v, z] + jnp.where((lane == 0) | (lane == 127), rolled, 0.0)
+        whole = cells[...] + jnp.where((lane == 0) | (lane == 127), rolled, 0.0)
         from_down = jnp.where(a > 0, recv_x[0, k : k + 1, :], 0.0)
         from_up = jnp.where(a < na - 1, recv_x[1, k : k + 1, :], 0.0)
-        dst[v, z, 8:120, :] = whole[8:120]
-        dst[v, z, 0:8, :] = whole[0:8] + jnp.where(row8 == 0, from_down, 0.0)
-        dst[v, z, 120:128, :] = whole[120:128] + jnp.where(row8 == 7, from_up, 0.0)
+        cells[8:120, :] = whole[8:120]
+        cells[0:8, :] = whole[0:8] + jnp.where(row8 == 0, from_down, 0.0)
+        cells[120:128, :] = whole[120:128] + jnp.where(row8 == 7, from_up, 0.0)
+
+    def transport(field, z):
+        u = field(z)
+        total = pltpu.roll(coef[0, z] * u, 1, 0) + pltpu.roll(coef[1, z] * u, 127, 0)
+        total = total + pltpu.roll(coef[2, z] * u, 1, 1) + pltpu.roll(coef[3, z] * u, 127, 1)
+        if z > 0:
+            total = total + coef[4, z] * field(z - 1)
+        if z < 3:
+            total = total + coef[5, z] * field(z + 1)
+        return total + 0.1 * u
 
     def advance(src, dst, v, z):
         u = src[v, z]
@@ -352,8 +382,8 @@
 
         lax.fori_loop(0, vs, one, 0)
 
-    near = [(v, z) for z in (0, 1) for v in range(8)] + [(7, 2)]
-    far = [(v, 2) for v in range(7)] + [(v, 3) for v in range(8)]
+    near = [(7, 0), (7, 1), (7, 2), (8, 0), (8, 1)]
+    far = [(v, z) for z in range(4) for v in range(7)] + [(7, 3)]
     faced = [(7, 0), (7, 1)]
     later = [(v, z) for z in range(4) for v in range(8) if (v, z) not in faced]
     first = (first_send_x, first_send_y, first_recv_x, first_recv_y)
@@ -377,7 +407,7 @@
         signal(ready.at[0], device(move))
 
     for z in (0, 1):
-        advance(u_ref, u1, 7, z)
+        u1[7, z] = transport(lambda at: u_ref[7, at], z) + 0.3 * q_ref[z]
     columns = jnp.zeros((128, 128), F32)
     for z in (0, 1):
         upper = 0.15 + 0.15 * w_ref[0, z, 120:128, :]
@@ -394,9 +424,9 @@
         columns = jnp.where(lane == 6 + z, pltpu.roll(factor, 6 + z, 1), columns)
     face_send_y[...] = columns.T[0:8, :]
     send_edges(1, *of_faces)
+    u1[7, 2] = transport(lambda at: u_ref[7, at], 2) + 0.3 * q_ref[2]
     for z in (0, 1):
-        advance_all(u_ref, u1, 7, z)
-    advance(u_ref, u1, 7, 2)
+        source_ref[z] = transport(lambda at: q_ref[at], z) + 0.3 * weighted(second, z)
     if y_moves:
         pl.semaphore_wait(ready.at[0], len(y_moves))
     for move in blk_moves:
@@ -414,14 +444,12 @@
     sel_t[...] = dot(sel, flip).astype(BF16)
     tile_high, tile_low = split(jnp.broadcast_to(tile_ref[...].astype(F32), (128, 256)).T)
     label_ref[...] = dot(sel, tile_high) + dot(sel, tile_low)
-    pack(u_ref, far, rest_send_x, rest_send_y)
-    send_edges(2, *rest)
 
     wait_edges(0, first_recv_x, first_recv_y)
     for k, (v, z) in enumerate(near):
-        mend(u1, first_recv_x, k, v, z)
+        mend(source_ref.at[z] if v == 8 else u1.at[v, z], first_recv_x, k)
     for z in (0, 1):
-        advance(u1, out_ref, 7, z)
+        out_ref[7, z] = transport(lambda at: u1[7, at], z) + 0.3 * source_ref[z]
 
     for side in range(2):
         take(face_recv_x.at[side], edge_sems.at[1, 1, side])
@@ -450,7 +478,7 @@
     beside = [from_right[0:1], from_left[0:1], from_right[1:2], from_left[1:2]]
     turned[...] = jnp.concatenate(beside + [jnp.zeros((124, 128), F32)], axis=0).T
     for k, (v, z) in enumerate(faced):
-        mend(out_ref, ring_x, k, v, z)
+        mend(out_ref.at[v, z], ring_x, k)
     current = out_ref[7, 1] - out_ref[7, 0]
 
     halves = [pltpu.roll(current, 64, 1).reshape(16, 8, 128), current.reshape(16, 8, 128)]
@@ -485,16 +513,12 @@
     pl.semaphore_wait(ready.at[1], len(blk_moves))
     send_all(face_send, face_recv, 0)
 
-    advance_all(u_ref, u1, 7, 2)
-    advance_all(u_ref, u1, 8, 3)
-    wait_edges(2, rest_recv_x, rest_recv_y)
-    for k, (v, z) in enumerate(far):
-        mend(u1, rest_recv_x, k, v, z)
-    pack(u1, later, last_send_x, last_send_y)
-    send_edges(3, *last)
-
-    fetches[2].wait()
     fetches[3].wait()
+    pack(u_ref, far, rest_send_x, rest_send_y)
+    send_edges(2, *rest)
+
+    fetches[4].wait()
+    fetches[5].wait()
 
     def per_row(column):
         return jnp.sum(
@@ -517,6 +541,9 @@
     base_high, base_low = split(rows_of(cosine, sine) * (1.0 / cols_total))
     base_ref[0] = base_high
     base_ref[1] = base_low
+
+    for z in range(3):
+        advance_all(u_ref, u1, 7, z)
 
     take(face_recv.at[pl.ds(0, count - 1)], recv_sems.at[0])
     got = face_recv[...].reshape(slots, 128)
@@ -561,7 +588,7 @@
         remote(spec_send.at[peer], spec_recv.at[b], send_sems.at[1], recv_sems.at[1], (a, peer))
     spec_recv[b] = spec_send[b]
 
-    fetches[4].wait()
+    fetches[6].wait()
     row_of_lane = a * lat + iota((PAIRS, lat), 1)
     x = -1.0 + (2.0 * row_of_lane.astype(F32) + 1.0) / rows_total
     log_sine = jnp.log(jnp.sqrt(1.0 - x * x))
@@ -604,16 +631,12 @@
     mask_ref[0] = jnp.where(mine & jnp.logical_not(is_high), scale, 0.0)
     mask_ref[1] = jnp.where(mine & is_high, scale, 0.0)
 
-    order_col, weight_col = per_row(64), per_row(65)
-    cosine, sine = waves()
-    weight = weight_col.reshape(nb, 2, 1, PAIRS, 1)
-    slope_weight = (weight_col * order_col).reshape(nb, 2, 1, PAIRS, 1)
-    value_high, value_low = split(rows_of(cosine * weight, sine * weight))
-    values_ref[0, :, 0:lon] = value_high
-    values_ref[1, :, 0:lon] = value_low
-    slope_high, slope_low = split(rows_of(-sine * slope_weight, cosine * slope_weight))
-    values_ref[0, :, lon : 2 * lon] = slope_high
-    values_ref[1, :, lon : 2 * lon] = slope_low
+    advance_all(u_ref, u1, 8, 3)
+    wait_edges(2, rest_recv_x, rest_recv_y)
+    for k, (v, z) in enumerate(far):
+        mend(u1.at[v, z], rest_recv_x, k)
+    pack(u1, later, last_send_x, last_send_y)
+    send_edges(3, *last)
 
     take(spec_recv.at[pl.ds(0, nb - 1)], recv_sems.at[1])
     spec = spec_recv[0]
@@ -666,11 +689,22 @@
             recv_sems.at[3],
             (a, peer_b[move[2:]]),
         )
+    order_col, weight_col = per_row(64), per_row(65)
+    cosine, sine = waves()
+    weight = weight_col.reshape(nb, 2, 1, PAIRS, 1)
+    slope_weight = (weight_col * order_col).reshape(nb, 2, 1, PAIRS, 1)
+    value_high, value_low = split(rows_of(cosine * weight, sine * weight))
+    values_ref[0, :, 0:lon] = value_high
+    values_ref[1, :, 0:lon] = value_low
+    slope_high, slope_low = split(rows_of(-sine * slope_weight, cosine * slope_weight))
+    values_ref[0, :, lon : 2 * lon] = slope_high
+    values_ref[1, :, lon : 2 * lon] = slope_low
+
     for z in (2, 3):
         advance_all(u1, out_ref, 8, z)
     wait_edges(3, last_recv_x, last_recv_y)
     for k, (v, z) in enumerate(later):
-        mend(out_ref, last_recv_x, k, v, z)
+        mend(out_ref.at[v, z], last_recv_x, k)
     take(syn_all.at[pl.ds(0, nb - 1)], recv_sems.at[3])
 
     syn_high, syn_middle, syn_low = split3(syn_all[...].reshape(spec_rows, lat).T)
@@ -699,7 +733,7 @@
     azimuthal = turned_slopes[0:lat] + (
         turned_slopes[lat:] + dot(syn_high, values_ref[1, :, lon : 2 * lon])
     )
-    fetches[5].wait()
+    fetches[7].wait()
     grid_row = iota((lat, 1), 0)
     global_row = a * lat + grid_row
     x_col = -1.0 + (2.0 * global_row.astype(F32) + 1.0) / rows_total
@@ -850,8 +884,10 @@
                 pltpu.VMEM((steps // 16 + 1, PAIRS, 128), F32),
                 pltpu.VMEM((7, 4, 128, 128), F32),
                 pltpu.VMEM((8, 4, 128, 128), F32),
-                *edges(24, 40),
-                *edges(16, 32),
+                pltpu.VMEM((3, 128, 128), F32),
+                pltpu.VMEM((2, 128, 128), F32),
+                *edges(8, 16),
+                *edges(32, 64),
                 *edges(8, 8),
                 pltpu.VMEM((2, 8, 128), F32),
                 pltpu.VMEM((8, 128), F32),
@@ -883,7 +919,7 @@
                 dma((5,)),
                 dma((2, 2)),
                 dma((2, 4)),
-                dma((7,)),
+                dma((8,)),
                 pltpu.SemaphoreType.REGULAR((2,)),
             ],
             compiler_params=pltpu.CompilerParams(

time: 61 us -> 61.1 us (level)
  no operation moved by 1% of the time
where the time goes in v1:
time: 61.1 us; the launch traced here: 60.9 us
  Pallas kernels  60.1 us (98%)
  between operations  0.8 us (1%)
    pallas_call x1, Pallas kernels, shards(): pl.pallas_call(functools.partial(kernel, (na, nb, steps)), out_shape=tupl...  58.5 us
    pallas_call x1, Pallas kernels, shards(): pl.pallas_call(write_out, out_shape=tuple((jax.ShapeDtypeStruct(shape, F3...  1.62 us

profile of v1, /device:TPU:1, one launch (start us, length us, event | category | flops | bytes accessed | tf_op | source)
XLA Modules:
  0.0 60.9 jit_solution(15247130509290441484)
XLA Ops:
  0.6 58.5 %shard_map.120 = (f32[8,4,128,128]{3,2,1,0:T(8,128)S(1)}, f32[256,256]{1,0:T(8,128)S(1)}, f32[256,256]{1,0:T(8,128)S(1)}, f32[256,128]{1,0:T(8,128)S(1)}) custom-call(f32[8,4,128,128]{3,2,1,0:T(8,128)} %u_hbm.1, f32[3,4,128,128]{3,2,1,0:T(8,128)} %w_hbm.1, f32[8,8]{1,0:T(8,128)} %mix_ref.1, f32[256,256]{1,0:T(8,128)} %ped_hbm.1, s32[1,256]{1,0:T(1,128)} %bitcast.2, ...), custom_call_target="tpu_custom_call" | custom-call | tf_op jit(solution)/shard_map/pallas_call | solution.py:863
  59.1 1.6 %shard_map.121 = (f32[8,4,128,128]{3,2,1,0:T(8,128)}, f32[256,256]{1,0:T(8,128)}, f32[256,256]{1,0:T(8,128)}, f32[256,128]{1,0:T(8,128)}) custom-call(f32[8,4,128,128]{3,2,1,0:T(8,128)S(1)} %get-tuple-element.8.slab, f32[256,256]{1,0:T(8,128)S(1)} %get-tuple-element.9.potential, f32[256,256]{1,0:T(8,128)S(1)} %get-tuple-element.10.heating, ...), custom_call_target="tpu_custom_call" | custom-call | tf_op jit(solution)/shard_map/pallas_call | solution.py:939

commit v2 on v1

--- a/solution.py
+++ b/solution.py
@@ -399,13 +399,6 @@
             corner_send[4 + 2 * side + z : 5 + 2 * side + z, :] = first_send_y[
                 2 * k + side : 2 * k + side + 1, :
             ]
-    pl.semaphore_wait(barrier, len(greeted))
-    send_edges(0, *first)
-    for at, target in enumerate(corners):
-        remote(corner_send, corner_recv.at[at], corner_sems.at[0, at], corner_sems.at[1, at], target)
-    for move in y_moves:
-        signal(ready.at[0], device(move))
-
     for z in (0, 1):
         u1[7, z] = transport(lambda at: u_ref[7, at], z) + 0.3 * q_ref[z]
     columns = jnp.zeros((128, 128), F32)
@@ -423,7 +416,13 @@
         columns = jnp.where(lane == 4 + z, pltpu.roll(scaled, 4 + z, 1), columns)
         columns = jnp.where(lane == 6 + z, pltpu.roll(factor, 6 + z, 1), columns)
     face_send_y[...] = columns.T[0:8, :]
+    pl.semaphore_wait(barrier, len(greeted))
     send_edges(1, *of_faces)
+    send_edges(0, *first)
+    for at, target in enumerate(corners):
+        remote(corner_send, corner_recv.at[at], corner_sems.at[0, at], corner_sems.at[1, at], target)
+    for move in y_moves:
+        signal(ready.at[0], device(move))
     u1[7, 2] = transport(lambda at: u_ref[7, at], 2) + 0.3 * q_ref[2]
     for z in (0, 1):
         source_ref[z] = transport(lambda at: q_ref[at], z) + 0.3 * weighted(second, z)
@@ -580,13 +579,22 @@
         forcing[0, pl.ds(r, 32, stride=8), :] = rows[:, 0:128]
         forcing[1, pl.ds(r, 32, stride=8), :] = rows[:, 128:256]
 
-    force = split(jnp.concatenate([forcing[0], forcing[1]], axis=1))
-    spectrum = dot3((base_ref[0], base_ref[1]), force, ((1,), (1,)))
-    spec_send[...] = spectrum.reshape(nb, 4 * PAIRS, lat)
-    for move in inner_moves:
-        peer = peer_b[move[2:]]
-        remote(spec_send.at[peer], spec_recv.at[b], send_sems.at[1], recv_sems.at[1], (a, peer))
-    spec_recv[b] = spec_send[b]
+    middle_row = lat // 2
+    for half in range(2):
+        rows = slice(half * middle_row, (half + 1) * middle_row)
+        force = split(jnp.concatenate([forcing[0, rows], forcing[1, rows]], axis=1))
+        spectrum = dot3((base_ref[0], base_ref[1]), force, ((1,), (1,)))
+        spec_send[half] = spectrum.reshape(nb, 4 * PAIRS, middle_row)
+        for move in inner_moves:
+            peer = peer_b[move[2:]]
+            remote(
+                spec_send.at[half, peer],
+                spec_recv.at[half, b],
+                send_sems.at[1 + 4 * half],
+                recv_sems.at[1 + 4 * half],
+                (a, peer),
+            )
+        spec_recv[half, b] = spec_send[half, b]
 
     fetches[6].wait()
     row_of_lane = a * lat + iota((PAIRS, lat), 1)
@@ -638,13 +646,17 @@
     pack(u1, later, last_send_x, last_send_y)
     send_edges(3, *last)
 
-    take(spec_recv.at[pl.ds(0, nb - 1)], recv_sems.at[1])
-    spec = spec_recv[0]
-    for at in range(1, nb):
-        spec = spec + spec_recv[at]
-    spec_high, spec_low = split(spec)
-    both = dot(jnp.concatenate([spec_high, spec_low], axis=0), leg[0], ((1,), (1,)))
-    wide_sums = both[0:32] + both[32:64] + dot(spec_high, leg[1], ((1,), (1,)))
+    wide_sums = None
+    for half in range(2):
+        take(spec_recv.at[half, pl.ds(0, nb - 1)], recv_sems.at[1 + 4 * half])
+        spec = spec_recv[half, 0]
+        for at in range(1, nb):
+            spec = spec + spec_recv[half, at]
+        spec_high, spec_low = split(spec)
+        cols = slice(half * middle_row, (half + 1) * middle_row)
+        both = dot(jnp.concatenate([spec_high, spec_low], axis=0), leg[0, :, cols], ((1,), (1,)))
+        part = both[0:32] + both[32:64] + dot(spec_high, leg[1, :, cols], ((1,), (1,)))
+        wide_sums = part if wide_sums is None else wide_sums + part
     for parity in range(2):
         low_rows = wide_sums[parity * 8 : parity * 8 + 8]
         high_rows = wide_sums[16 + parity * 8 : 24 + parity * 8]
@@ -680,15 +692,18 @@
     fine = dot(solved_high, leg[2])
     both = dot(solved_both, leg[0])
     middle = dot(solved_both, leg[1])
-    syn_all[b] = both[0:32] + (both[32:64] + (middle[0:32] + (middle[32:64] + fine)))
-    for move in inner_moves:
-        remote(
-            syn_all.at[b],
-            syn_all.at[b],
-            send_sems.at[3],
-            recv_sems.at[3],
-            (a, peer_b[move[2:]]),
-        )
+    syn = both[0:32] + (both[32:64] + (middle[0:32] + (middle[32:64] + fine)))
+    for half in range(2):
+        syn_all[half, b] = syn[:, half * middle_row : (half + 1) * middle_row]
+    for half in range(2):
+        for move in inner_moves:
+            remote(
+                syn_all.at[half, b],
+                syn_all.at[half, b],
+                send_sems.at[3 + 3 * half],
+                recv_sems.at[3 + 3 * half],
+                (a, peer_b[move[2:]]),
+            )
     order_col, weight_col = per_row(64), per_row(65)
     cosine, sine = waves()
     weight = weight_col.reshape(nb, 2, 1, PAIRS, 1)
@@ -705,9 +720,6 @@
     wait_edges(3, last_recv_x, last_recv_y)
     for k, (v, z) in enumerate(later):
         mend(out_ref.at[v, z], last_recv_x, k)
-    take(syn_all.at[pl.ds(0, nb - 1)], recv_sems.at[3])
-
-    syn_high, syn_middle, syn_low = split3(syn_all[...].reshape(spec_rows, lat).T)
 
     def potential_of(high, middle, low):
         rows = high.shape[0]
@@ -717,22 +729,26 @@
             coarse[rows : 2 * rows] + (rest_of[0:rows] + (coarse[2 * rows :] + rest_of[rows:]))
         )
 
-    def rims_of(part):
-        return jnp.concatenate([part[0:16], part[lat - 16 :]], axis=0)
-
-    rims = potential_of(rims_of(syn_high), rims_of(syn_middle), rims_of(syn_low))
-    rim_send[0] = rims[0:8]
-    rim_send[1] = rims[24:32]
-    remote(rim_send.at[1], rim_recv.at[0], rim_sems.at[0, 0], rim_sems.at[1, 0], (up_a, b))
-    remote(rim_send.at[0], rim_recv.at[1], rim_sems.at[0, 1], rim_sems.at[1, 1], (down_a, b))
-    potential = potential_of(syn_high, syn_middle, syn_low)
+    potentials, slopes = [], []
+    for half, target in enumerate(((down_a, b), (up_a, b))):
+        take(syn_all.at[half, pl.ds(0, nb - 1)], recv_sems.at[3 + 3 * half])
+        parts = split3(syn_all[half].reshape(spec_rows, middle_row).T)
+        rims = potential_of(*(part[0:16] if half == 0 else part[middle_row - 16 :] for part in parts))
+        rim_send[half] = rims[0:8] if half == 0 else rims[8:16]
+        remote(
+            rim_send.at[half],
+            rim_recv.at[1 - half],
+            rim_sems.at[0, half],
+            rim_sems.at[1, 1 - half],
+            target,
+        )
+        potentials.append(potential_of(*parts))
+        coarse = dot(jnp.concatenate(parts[0:2], axis=0), values_ref[0, :, lon : 2 * lon])
+        finer = dot(parts[0], values_ref[1, :, lon : 2 * lon])
+        slopes.append(coarse[0:middle_row] + (coarse[middle_row:] + finer))
+    potential = jnp.concatenate(potentials, axis=0)
+    azimuthal = jnp.concatenate(slopes, axis=0)
     pot_ref[...] = potential
-    turned_slopes = dot(
-        jnp.concatenate([syn_high, syn_middle], axis=0), values_ref[0, :, lon : 2 * lon]
-    )
-    azimuthal = turned_slopes[0:lat] + (
-        turned_slopes[lat:] + dot(syn_high, values_ref[1, :, lon : 2 * lon])
-    )
     fetches[7].wait()
     grid_row = iota((lat, 1), 0)
     global_row = a * lat + grid_row
@@ -813,14 +829,15 @@
     for at, (sent_x, sent_y, _, _) in enumerate((first, of_faces, rest, last)):
         drain_edges(at, sent_x, sent_y)
     take(face_send.at[pl.ds(0, count - 1)], send_sems.at[0])
-    take(spec_send.at[pl.ds(0, nb - 1)], send_sems.at[1])
+    for half in range(2):
+        take(spec_send.at[half, pl.ds(0, nb - 1)], send_sems.at[1 + 4 * half])
+        take(syn_all.at[half, pl.ds(0, nb - 1)], send_sems.at[3 + 3 * half])
     take(coef_recv.at[pl.ds(0, na - 1)], send_sems.at[2])
-    take(syn_all.at[pl.ds(0, nb - 1)], send_sems.at[3])
     take(reply_send.at[pl.ds(0, count - 1)], send_sems.at[4])
     for at in range(4):
         take(corner_send, corner_sems.at[0, at])
-    take(rim_send.at[0], rim_sems.at[0, 1])
-    take(rim_send.at[1], rim_sems.at[0, 0])
+    take(rim_send.at[0], rim_sems.at[0, 0])
+    take(rim_send.at[1], rim_sems.at[0, 1])
 
 
 def write_out(slab, potential, heating, blocks, *refs):
@@ -901,13 +918,13 @@
                 pltpu.VMEM((2, lat, 128), F32),
                 pltpu.VMEM((2, 2 * orders, lon), BF16),
                 pltpu.VMEM((2, 2 * orders, 2 * lon), BF16),
-                pltpu.VMEM((nb, 4 * PAIRS, lat), F32),
-                pltpu.VMEM((nb, 4 * PAIRS, lat), F32),
+                pltpu.VMEM((2, nb, 4 * PAIRS, lat // 2), F32),
+                pltpu.VMEM((2, nb, 4 * PAIRS, lat // 2), F32),
                 pltpu.VMEM((3, width, lat), BF16),
                 pltpu.VMEM((2, PAIRS, width), F32),
                 pltpu.VMEM((2, width), F32),
                 pltpu.VMEM((na, 2, width), F32),
-                pltpu.VMEM((nb, 4 * PAIRS, lat), F32),
+                pltpu.VMEM((2, nb, 4 * PAIRS, lat // 2), F32),
                 pltpu.VMEM((2, 8, lon), F32),
                 pltpu.VMEM((2, 8, lon), F32),
                 pltpu.VMEM((4, lat, 128), F32),
@@ -915,8 +932,8 @@
                 pltpu.VMEM((count, cap, 128), F32),
                 pltpu.VMEM((count, cap, 128), F32),
                 dma((2, 4, 4)),
-                dma((5,)),
-                dma((5,)),
+                dma((7,)),
+                dma((7,)),
                 dma((2, 2)),
                 dma((2, 4)),
                 dma((8,)),

time: 61.1 us -> 59.9 us (0.980)
  Pallas kernels: 60.1 us -> 59 us
    pallas_call x1, Pallas kernels: 58.5 us -> 57.3 us  [shards(): pl.pallas_call(functools.partial(kernel, (na, nb, steps)), out_shape=tupl...]
where the time goes in v2:
time: 59.9 us; the launch traced here: 59.8 us
  Pallas kernels  59 us (98%)
  between operations  0.8 us (1%)
    pallas_call x1, Pallas kernels, shards(): pl.pallas_call(functools.partial(kernel, (na, nb, steps)), out_shape=tupl...  57.3 us
    pallas_call x1, Pallas kernels, shards(): pl.pallas_call(write_out, out_shape=tuple((jax.ShapeDtypeStruct(shape, F3...  1.62 us

profile of v2, /device:TPU:1, one launch (start us, length us, event | category | flops | bytes accessed | tf_op | source)
XLA Modules:
  0.0 59.8 jit_solution(16330178481347366906)
XLA Ops:
  0.6 57.3 %shard_map.120 = (f32[8,4,128,128]{3,2,1,0:T(8,128)S(1)}, f32[256,256]{1,0:T(8,128)S(1)}, f32[256,256]{1,0:T(8,128)S(1)}, f32[256,128]{1,0:T(8,128)S(1)}) custom-call(f32[8,4,128,128]{3,2,1,0:T(8,128)} %u_hbm.1, f32[3,4,128,128]{3,2,1,0:T(8,128)} %w_hbm.1, f32[8,8]{1,0:T(8,128)} %mix_ref.1, f32[256,256]{1,0:T(8,128)} %ped_hbm.1, s32[1,256]{1,0:T(1,128)} %bitcast.2, ...), custom_call_target="tpu_custom_call" | custom-call | tf_op jit(solution)/shard_map/pallas_call | solution.py:880
  58.0 1.6 %shard_map.121 = (f32[8,4,128,128]{3,2,1,0:T(8,128)}, f32[256,256]{1,0:T(8,128)}, f32[256,256]{1,0:T(8,128)}, f32[256,128]{1,0:T(8,128)}) custom-call(f32[8,4,128,128]{3,2,1,0:T(8,128)S(1)} %get-tuple-element.8.slab, f32[256,256]{1,0:T(8,128)S(1)} %get-tuple-element.9.potential, f32[256,256]{1,0:T(8,128)S(1)} %get-tuple-element.10.heating, ...), custom_call_target="tpu_custom_call" | custom-call | tf_op jit(solution)/shard_map/pallas_call | solution.py:956

commit v3 on v2

--- a/solution.py
+++ b/solution.py
@@ -579,10 +579,14 @@
         forcing[0, pl.ds(r, 32, stride=8), :] = rows[:, 0:128]
         forcing[1, pl.ds(r, 32, stride=8), :] = rows[:, 128:256]
 
-    middle_row = lat // 2
+    middle_row, quarter = lat // 2, lat // 4
     for half in range(2):
-        rows = slice(half * middle_row, (half + 1) * middle_row)
-        force = split(jnp.concatenate([forcing[0, rows], forcing[1, rows]], axis=1))
+        whole = [forcing[0], forcing[1]]
+        if half == 0:
+            rows = [jnp.concatenate([part[0:quarter], part[lat - quarter :]], axis=0) for part in whole]
+        else:
+            rows = [part[quarter : lat - quarter] for part in whole]
+        force = split(jnp.concatenate(rows, axis=1))
         spectrum = dot3((base_ref[0], base_ref[1]), force, ((1,), (1,)))
         spec_send[half] = spectrum.reshape(nb, 4 * PAIRS, middle_row)
         for move in inner_moves:
@@ -597,7 +601,13 @@
         spec_recv[half, b] = spec_send[half, b]
 
     fetches[6].wait()
-    row_of_lane = a * lat + iota((PAIRS, lat), 1)
+    place = iota((PAIRS, lat), 1)
+    place = jnp.where(
+        place < quarter,
+        place,
+        jnp.where(place < middle_row, place + middle_row, place - quarter),
+    )
+    row_of_lane = a * lat + place
     x = -1.0 + (2.0 * row_of_lane.astype(F32) + 1.0) / rows_total
     log_sine = jnp.log(jnp.sqrt(1.0 - x * x))
     turns = steps // 16
@@ -730,24 +740,33 @@
         )
 
     potentials, slopes = [], []
-    for half, target in enumerate(((down_a, b), (up_a, b))):
+    for half in range(2):
         take(syn_all.at[half, pl.ds(0, nb - 1)], recv_sems.at[3 + 3 * half])
         parts = split3(syn_all[half].reshape(spec_rows, middle_row).T)
-        rims = potential_of(*(part[0:16] if half == 0 else part[middle_row - 16 :] for part in parts))
-        rim_send[half] = rims[0:8] if half == 0 else rims[8:16]
-        remote(
-            rim_send.at[half],
-            rim_recv.at[1 - half],
-            rim_sems.at[0, half],
-            rim_sems.at[1, 1 - half],
-            target,
-        )
+        if half == 0:
+            rims = potential_of(
+                *(jnp.concatenate([part[0:16], part[middle_row - 16 :]], axis=0) for part in parts)
+            )
+            rim_send[0] = rims[0:8]
+            rim_send[1] = rims[24:32]
+            for side, target in enumerate(((down_a, b), (up_a, b))):
+                remote(
+                    rim_send.at[side],
+                    rim_recv.at[1 - side],
+                    rim_sems.at[0, side],
+                    rim_sems.at[1, 1 - side],
+                    target,
+                )
         potentials.append(potential_of(*parts))
         coarse = dot(jnp.concatenate(parts[0:2], axis=0), values_ref[0, :, lon : 2 * lon])
         finer = dot(parts[0], values_ref[1, :, lon : 2 * lon])
         slopes.append(coarse[0:middle_row] + (coarse[middle_row:] + finer))
-    potential = jnp.concatenate(potentials, axis=0)
-    azimuthal = jnp.concatenate(slopes, axis=0)
+
+    def in_order(outer, inner):
+        return jnp.concatenate([outer[0:quarter], inner, outer[quarter:]], axis=0)
+
+    potential = in_order(*potentials)
+    azimuthal = in_order(*slopes)
     pot_ref[...] = potential
     fetches[7].wait()
     grid_row = iota((lat, 1), 0)

time: 59.9 us -> 59.6 us (level)
  no operation moved by 1% of the time
where the time goes in v3:
time: 59.6 us; the launch traced here: 59.4 us
  Pallas kernels  58.6 us (98%)
  between operations  0.8 us (1%)
    pallas_call x1, Pallas kernels, shards(): pl.pallas_call(functools.partial(kernel, (na, nb, steps)), out_shape=tupl...  57 us
    pallas_call x1, Pallas kernels, shards(): pl.pallas_call(write_out, out_shape=tuple((jax.ShapeDtypeStruct(shape, F3...  1.62 us

profile of v3, /device:TPU:1, one launch (start us, length us, event | category | flops | bytes accessed | tf_op | source)
XLA Modules:
  0.0 59.4 jit_solution(15620481129073073921)
XLA Ops:
  0.6 57.0 %shard_map.120 = (f32[8,4,128,128]{3,2,1,0:T(8,128)S(1)}, f32[256,256]{1,0:T(8,128)S(1)}, f32[256,256]{1,0:T(8,128)S(1)}, f32[256,128]{1,0:T(8,128)S(1)}) custom-call(f32[8,4,128,128]{3,2,1,0:T(8,128)} %u_hbm.1, f32[3,4,128,128]{3,2,1,0:T(8,128)} %w_hbm.1, f32[8,8]{1,0:T(8,128)} %mix_ref.1, f32[256,256]{1,0:T(8,128)} %ped_hbm.1, s32[1,256]{1,0:T(1,128)} %bitcast.2, ...), custom_call_target="tpu_custom_call" | custom-call | tf_op jit(solution)/shard_map/pallas_call | solution.py:899
  57.7 1.6 %shard_map.121 = (f32[8,4,128,128]{3,2,1,0:T(8,128)}, f32[256,256]{1,0:T(8,128)}, f32[256,256]{1,0:T(8,128)}, f32[256,128]{1,0:T(8,128)}) custom-call(f32[8,4,128,128]{3,2,1,0:T(8,128)S(1)} %get-tuple-element.8.slab, f32[256,256]{1,0:T(8,128)S(1)} %get-tuple-element.9.potential, f32[256,256]{1,0:T(8,128)S(1)} %get-tuple-element.10.heating, ...), custom_call_target="tpu_custom_call" | custom-call | tf_op jit(solution)/shard_map/pallas_call | solution.py:975
